TPU v7x, 32 devices: a whole 2x2x4 slice. The times are simulated.
32 devices in a mesh: row: 16 (over z, y, x), col: 2 (over core).
Axes of the slice: x: 2, y: 2, z: 4, core: 2. Of those that a mesh axis runs over, the one named last changes fastest.
Arguments:
- top_inverse: float32 [2, 1024, 1024], P(None, 'row', 'col'), may hold values from -6 to 6, as said below
- blocks_upper: int32 [2, 2], replicated, may hold values from 0 to 3, as said below
- factor_upper: float32 [2, 2, 512, 4096], P(None, None, 'row', 'col'), may hold values from -0.1875 to 0.1875
- diagonal_upper: float32 [2, 2, 4096, 4096], P(None, None, 'row', 'col'), may hold values from -6 to 6, as said below
- parents_lower: int32 [3], replicated, may hold values from 0 to 1
- blocks_lower: int32 [3, 2], replicated, may hold values from 0 to 15, as said below
- factor_lower: float32 [3, 2, 512, 4096], P(None, None, 'row', 'col'), may hold values from -0.1875 to 0.1875
- diagonal_lower: float32 [3, 2, 4096, 4096], P(None, None, 'row', 'col'), may hold values from -6 to 6, as said below
Outputs:
- coupling_inverse_upper: float32 [2, 2, 4096, 512], P(None, None, 'row')
- block_inverse_upper: float32 [2, 2, 4096, 4096], P(None, None, 'row', 'col')
- coupling_inverse_lower: float32 [3, 2, 4096, 512], P(None, None, 'row')
- block_inverse_lower: float32 [3, 2, 4096, 4096], P(None, None, 'row', 'col')
Inputs may be any that keep to these rules, and one draw needn't show every extreme that they name: `top_inverse`: equal to its own transpose (no conjugation) in both parts. `diagonal_upper`: each matrix equals its own transpose (no conjugation) in both parts. `diagonal_lower`: each matrix equals its own transpose (no conjugation) in both parts. `blocks_upper`: each row names 2 different blocks. `blocks_lower`: each row names 2 different blocks.
All inputs are finite; a program needn't handle non-finite values.
Results may differ from a plain program's by a relative error of at most 0.00011.
Values sent between devices are 32-bit elements; how exact they have to be, the bound alone decides.
A program may use at most 256 MiB of HBM per device.

v0:
```python
import jax
import jax.numpy as jnp
from jax import lax
from jax.sharding import PartitionSpec as P

BS = 256
KB = 16
NB = 2
NTB = 4
UPPER = 2


def from_root(block, axis, source):
    block = jnp.where(lax.axis_index(axis) == source, block, jnp.zeros_like(block))
    return lax.psum(block, axis)


def complex_product(first_side, second_side, pattern):
    pieces_all = jnp.einsum(
        pattern,
        first_side,
        second_side,
        precision=lax.Precision.HIGHEST,
        preferred_element_type=jnp.float32,
    )
    real_part = pieces_all[:, 0, 0] - pieces_all[:, 1, 1]
    imag_part = pieces_all[:, 0, 1] + pieces_all[:, 1, 0]
    return jnp.stack([real_part, imag_part], axis=1)


def pick_blocks(stacked, blocks, blocks_total, rows_within, cols_within):
    batch_size = stacked.shape[0]
    tiled_view = stacked.reshape(
        batch_size, 2, rows_within, blocks_total, cols_within, blocks_total
    )

    def pick_single(matrix, chosen):
        matrix = jnp.take(matrix, chosen, axis=2)
        matrix = jnp.take(matrix, chosen, axis=4)
        return matrix.reshape(2, rows_within * NB, cols_within * NB)

    return jax.vmap(pick_single)(tiled_view, blocks)


def supernode_level(chosen, factor_rows, diag_block, slice_start, root_col):
    gathered_factor = lax.all_gather(factor_rows, "row", axis=2, tiled=True)
    factor_columns = lax.dynamic_slice_in_dim(gathered_factor, slice_start, diag_block.shape[2], 3)
    factor_slice = from_root(factor_columns, "col", root_col)
    zeroes = jnp.zeros(
        factor_slice.shape[:2] + (factor_slice.shape[3], chosen.shape[3]), jnp.float32
    )
    factor_part = factor_slice
    coupled_part = zeroes - complex_product(
        factor_part, lax.all_gather(chosen, "row", axis=2, tiled=True), "bikm,bjkn->bijmn"
    )
    incoming = lax.all_gather(coupled_part, "col", axis=3, tiled=True)
    block_total = diag_block
    factor_part = gathered_factor
    block_total = block_total - complex_product(incoming, factor_part, "bimk,bjkn->bijmn")
    gathered = incoming
    block_total, gathered = (block_total, gathered)
    return (gathered, block_total)


def shards(
    top_inverse,
    blocks_upper,
    factor_upper,
    diagonal_upper,
    parents_lower,
    blocks_lower,
    factor_lower,
    diagonal_lower,
):
    row_devices = lax.axis_size("row")
    col_devices = lax.axis_size("col")
    rows_within = BS // row_devices
    cols_within = BS // col_devices
    ratio_axes = row_devices // col_devices
    my_row = lax.axis_index("row")
    root_col = my_row // ratio_axes
    slice_start = my_row % ratio_axes * rows_within * KB
    upper_spans = (0, UPPER)
    first_index, last_index = upper_spans
    width_now = last_index - first_index
    source = jnp.broadcast_to(top_inverse, (width_now,) + top_inverse.shape)
    chosen = pick_blocks(source, blocks_upper, NTB, rows_within, cols_within)
    coupling_out, block_out = supernode_level(
        chosen, factor_upper, diagonal_upper, slice_start, root_col
    )
    upper_coupling = coupling_out
    upper_blocks = block_out
    source = jnp.take(upper_blocks, parents_lower, axis=0)
    chosen = pick_blocks(source, blocks_lower, KB, rows_within, cols_within)
    coupling_out, block_out = supernode_level(
        chosen, factor_lower, diagonal_lower, slice_start, root_col
    )
    return (upper_coupling, upper_blocks, coupling_out, block_out)


def solution(mesh):
    placed = (
        P(None, "row", "col"),
        P(),
        P(None, None, "row", "col"),
        P(None, None, "row", "col"),
        P(),
        P(),
        P(None, None, "row", "col"),
        P(None, None, "row", "col"),
    )
    return jax.shard_map(
        shards,
        mesh=mesh,
        in_specs=placed,
        out_specs=(
            P(None, None, "row", None),
            P(None, None, "row", "col"),
            P(None, None, "row", None),
            P(None, None, "row", "col"),
        ),
        check_vma=False,
    )
```

profile of v0, /device:TPU:0, one launch (start us, length us, event | category | flops | bytes accessed | tf_op | source)
XLA Modules:
  0.0 991.6 jit_solution(4863785366521610066)
XLA Ops:
  8.7 10.8 %broadcast_in_dim.86 = f32[2,16,4,128,4]{4,3,2,1,0:T(8,128)} reshape(f32[2,64,512]{2,1,0:T(8,128)} %param.8) | data formatting | bytes 524288 | tf_op jit(solution)/shard_map/broadcast_in_dim | solution.py:86
  31.2 7.0 gather.28
  39.1 165.9 %all-gather.9.cloned.1.call-done = f32[2,2,512,2048]{3,2,1,0:T(8,128)} async-done(((f32[2,2,32,2048]{3,2,1,0:T(8,128)}), f32[2,2,512,2048]{3,2,1,0:T(8,128)}) %all-gather.9.cloned.1.call-update) | async-done | bytes 16777232 | tf_op jit(solution)/shard_map/all_gather | solution.py:46
  208.0 268.8 %all-gather.15.cloned.1.call-done = f32[3,2,512,2048]{3,2,1,0:T(8,128)} async-done(((f32[3,2,32,2048]{3,2,1,0:T(8,128)}), f32[3,2,512,2048]{3,2,1,0:T(8,128)}) %all-gather.15.cloned.1.call-update) | async-done | bytes 25165840 | tf_op jit(solution)/shard_map/all_gather | solution.py:46
  480.8 58.5 %all-gather.7.cloned.1.call-done = f32[2,2,512,256]{3,2,1,0:T(8,128)} async-done(((f32[2,2,32,256]{3,2,1,0:T(8,128)}), f32[2,2,512,256]{3,2,1,0:T(8,128)}) %all-gather.7.cloned.1.call-update) | async-done | bytes 2097168 | tf_op jit(solution)/shard_map/all_gather | solution.py:54
  539.2 32.0 %all-reduce.3.cloned.1.call-done = (f32[2,2,512,256]{3,2,1,0:T(8,128)}, f32[3,2,512,256]{3,2,1,0:T(8,128)}) async-done(((f32[2,2,512,256]{3,2,1,0:T(8,128)}, f32[3,2,512,256]{3,2,1,0:T(8,128)}), (f32[2,2,512,256]{3,2,1,0:T(8,128)}, f32[3,2,512,256]{3,2,1,0:T(8,128)})) %all-reduce.3.cloned.1.call-update) | async-done | bytes 5242896 | tf_op jit(solution)/shard_map/psum | solution.py:15
  579.5 10.6 %all-gather.11.cloned.1.call-done = f32[2,2,256,512]{2,3,0,1:T(8,128)} async-done(((f32[2,2,256,256]{2,3,0,1:T(8,128)}), f32[2,2,256,512]{2,3,0,1:T(8,128)}) %all-gather.11.cloned.1.call-update) | async-done | bytes 2097168 | tf_op jit(solution)/shard_map/all_gather | solution.py:56
  590.0 32.2 %fusion.7 = f32[2,2,2,256,2048]{4,3,2,1,0:T(8,128)S(1)} fusion(f32[2,2,512,2048]{3,2,1,0:T(8,128)} %all-gather.9.cloned.1.call-done, f32[2,2,256,512]{2,3,0,1:T(8,128)} %all-gather.11.cloned.1.call-done), kind=kOutput, calls=%fused_computation.15 | convolution fusion | flops 25769803776 | bytes 35651584 | tf_op jit(solution)/shard_map/bimk,bjkn->bijmn/dot_general | solution.py:19
  634.0 5.8 gather_fusion.5
  645.7 11.6 %pad_maximum_fusion = f32[3,2,256,2048]{3,2,1,0:T(8,128)} fusion(f32[3,2,256,1024]{3,2,1,0:T(8,128)} %gather_fusion.5, f32[3,2,256,1024]{3,2,1,0:T(8,128)} %gather_fusion.4), kind=kLoop, calls=%fused_computation.11 | loop fusion | flops 3145728 | bytes 25165824
  657.2 53.2 %gather.30 = f32[3,2,16,16,128,16]{5,4,3,2,1,0:T(8,128)} reshape(f32[3,2,256,2048]{3,2,1,0:T(8,128)} %pad_maximum_fusion) | data formatting | bytes 25165824 | tf_op jit(solution)/shard_map/jit(_take)/gather | solution.py:93
  710.5 64.7 %broadcast_select_fusion = f32[3,2,16,16,128,16]{5,4,3,2,1,0:T(8,128)} fusion(f32[3,2,16,16,128,16]{5,4,3,2,1,0:T(8,128)} %gather.30, pred[3]{0:T(512)(128)(4,1)S(1)} %compare_and_fusion), kind=kLoop, calls=%fused_computation.6 | loop fusion | flops 3145728 | bytes 25165828 | tf_op jit(solution)/shard_map/jit(_take)/select_n | solution.py:93
  775.2 11.1 %gather_fusion.2 = f32[6,2,16,128,16]{4,3,2,1,0:T(8,128)} fusion(f32[3,2,16,16,128,16]{5,4,3,2,1,0:T(8,128)} %broadcast_select_fusion, s32[6]{0:T(128)S(1)} %reshape.189), kind=kCustom, calls=%fused_computation.2 | custom fusion | bytes 3145776 | tf_op jit(solution)/shard_map/vmap(jit(_take))/gather | solution.py:38
  786.3 7.6 copy.89
  794.8 6.6 copy.90
  801.4 10.0 %gather.33 = f32[3,2,32,256]{3,2,1,0:T(8,128)S(1)} reshape(f32[3,2,16,2,128,2]{5,4,3,2,1,0:T(8,128)} %copy.90) | data formatting | bytes 393216 | tf_op jit(solution)/shard_map/vmap(jit(_take))/gather | solution.py:39
  812.2 69.7 %all-gather.13.cloned.1.call-done = f32[3,2,512,256]{3,2,1,0:T(8,128)} async-done(((f32[3,2,32,256]{3,2,1,0:T(8,128)}), f32[3,2,512,256]{3,2,1,0:T(8,128)}) %all-gather.13.cloned.1.call-update) | async-done | bytes 3145744 | tf_op jit(solution)/shard_map/all_gather | solution.py:54
  881.8 7.2 fusion.24
  890.6 8.6 copy.98
  901.7 45.8 %fusion.4 = f32[3,2,2,256,2048]{4,3,2,1,0:T(8,128)} fusion(f32[3,2,512,2048]{3,2,1,0:T(8,128)} %all-gather.15.cloned.1.call-done, f32[3,2,256,512]{2,3,0,1:T(8,128)} %all-gather.17.cloned.1.call-done), kind=kOutput, calls=%fused_computation.13 | convolution fusion | flops 38654705664 | bytes 53477376 | tf_op jit(solution)/shard_map/bimk,bjkn->bijmn/dot_general | solution.py:19
  947.5 5.9 fusion.10
  953.4 5.9 fusion.12
  959.3 10.9 %maximum_subtract_fusion = f32[3,2,256,2048]{3,2,0,1:T(8,128)} fusion(f32[3,1,256,2048]{3,2,0,1:T(8,128)S(1)} %fusion.10, f32[3,1,256,2048]{3,2,0,1:T(8,128)S(1)} %fusion.12, f32[3,2,256,2048]{3,2,1,0:T(8,128)} %param.15), kind=kLoop, calls=%fused_computation.12 | loop fusion | flops 6291456 | bytes 37748736 | tf_op jit(solution)/shard_map/sub | solution.py:59
  970.3 11.7 %copy.100 = f32[3,2,256,2048]{3,2,1,0:T(8,128)} copy(f32[3,2,256,2048]{3,2,0,1:T(8,128)} %maximum_subtract_fusion) | data formatting | bytes 25165824
  (72 shorter events, 54.7 us)
Async XLA Ops:
  7.2 197.8 %all-gather.9.cloned.1.call-start = ((), (), s32[]{:S(2)}) async-start(), calls=%async_computation.1 | async-start | bytes 17825792 | tf_op jit(solution)/shard_map/all_gather | solution.py:46
  7.9 468.9 %all-gather.15.cloned.1.call-start = ((), (), s32[]{:S(2)}) async-start(), calls=%async_computation.4 | async-start | bytes 26738688 | tf_op jit(solution)/shard_map/all_gather | solution.py:46
  8.6 530.6 %all-gather.7.cloned.1.call-start = ((), (), s32[]{:S(2)}) async-start(), calls=%async_computation | async-start | bytes 2228224 | tf_op jit(solution)/shard_map/all_gather | solution.py:54
  19.5 5.6 copy-start.5
  39.0 532.2 %all-reduce.3.cloned.1.call-start = ((), (), s32[]{:S(2)}) async-start(), calls=%async_computation.6 | async-start | bytes 10485760 | tf_op jit(solution)/shard_map/psum | solution.py:15
  480.7 109.3 %all-gather.11.cloned.1.call-start = ((), (), s32[]{:S(2)}) async-start(), calls=%async_computation.2 | async-start | bytes 3145728 | tf_op jit(solution)/shard_map/all_gather | solution.py:56
  571.2 7.2 copy-start.6
  571.2 8.3 copy-start.7
  578.2 303.7 %all-gather.13.cloned.1.call-start = ((), (), s32[]{:S(2)}) async-start(), calls=%async_computation.3 | async-start | bytes 3342336 | tf_op jit(solution)/shard_map/all_gather | solution.py:54
  628.3 5.7 copy-start
  801.4 10.0 %copy-start.4 = (pred[3,256]{1,0:T(4,128)(4,1)S(1)}, pred[3,256]{1,0:T(4,128)(4,1)}, u32[]{:S(2)}) copy-start(pred[3,256]{1,0:T(4,128)(4,1)} %broadcast_in_dim.94) | copy-start | bytes 2308
  801.4 80.4 %copy-start.3 = (f32[3,2,512,256]{3,2,1,0:T(8,128)S(1)}, f32[3,2,512,256]{3,2,1,0:T(8,128)}, u32[]{:S(2)}) copy-start(f32[3,2,512,256]{3,2,1,0:T(8,128)} %get-tuple-element.21) | copy-start | bytes 9437188
  812.1 89.6 %all-gather.17.cloned.1.call-start = ((), (), s32[]{:S(2)}) async-start(), calls=%async_computation.5 | async-start | bytes 4718592 | tf_op jit(solution)/shard_map/all_gather | solution.py:56
  890.6 8.6 copy-start.2
  970.3 11.7 %copy-start.1 = (f32[3,2,256,512]{2,3,0,1:T(8,128)S(1)}, f32[3,2,256,512]{2,3,0,1:T(8,128)}, u32[]{:S(2)}) copy-start(f32[3,2,256,512]{2,3,0,1:T(8,128)} %all-gather.17.cloned.1.call-done) | copy-start | bytes 9437188
Sparse Core Ops, SparseCore 0:
  10.8 194.1 all-gather.8
  207.7 269.0 all-gather.14
  480.1 59.0 all-gather.6
  542.2 28.9 all-reduce.2
  578.3 11.7 all-gather.10
  812.2 69.5 all-gather.12
  890.7 10.9 all-gather.16
where the time goes:
time: 999 us; the launch traced here: 992 us
  waiting for transfers between devices  607 us (61%)
  local copies, waits for them, and re-layouts  162 us (16%)
  other arithmetic  116 us (12%)
  matrix products  91.1 us (9%)
  between operations  14.8 us (1%)
    all_gather x2, waiting for transfers between devices, supernode_level(): gathered_factor = lax.all_gather(factor_rows, 'row', axis=2, tiled=True)  435 us
    all_gather x2, waiting for transfers between devices, supernode_level(): lax.all_gather(chosen, 'row', axis=2, tiled=True)  128 us
    dot_general x4, matrix products, complex_product(): jnp.einsum(pattern, first_side, second_side, precision=lax.Precision.HIGH...  91.1 us
    gather x4, local copies, waits for them, and re-layouts, shards(): source = jnp.take(upper_blocks, parents_lower, axis=0)  69.4 us
    select_n x2, other arithmetic, shards(): source = jnp.take(upper_blocks, parents_lower, axis=0)  64.7 us
    psum x1, waiting for transfers between devices, from_root(): return lax.psum(block, axis)  32 us
    gather x6, local copies, waits for them, and re-layouts, pick_single(): matrix = jnp.take(matrix, chosen, axis=4)  29.3 us
    unnamed x20, local copies, waits for them, and re-layouts  25.9 us
  transfers between devices with their start and end apart: 7, of which 7 were waited for; matrix products, arithmetic and copies ran while one was open for 5% of the time, Pallas kernels for 0%

commit v1 on v0

v1 whole, which is shorter than its diff:
```python
import jax
import jax.numpy as jnp
from jax import lax
from jax.sharding import PartitionSpec as P

HIGH = lax.Precision.HIGH
EXACT = lax.Precision.HIGHEST


def one_hot_rows(blocks, blocks_total, inner):
    chosen_blocks = blocks.shape[1]
    rows = lax.broadcasted_iota(jnp.int32, (inner * chosen_blocks, inner * blocks_total), 0)
    cols = lax.broadcasted_iota(jnp.int32, (inner * chosen_blocks, inner * blocks_total), 1)
    same = rows // chosen_blocks == cols // blocks_total
    wanted = jnp.zeros((blocks.shape[0],) + rows.shape, jnp.int32)
    for b in range(chosen_blocks):
        wanted = jnp.where(rows % chosen_blocks == b, blocks[:, b, None, None], wanted)
    return jnp.where(same & (cols % blocks_total == wanted), 1.0, 0.0).astype(jnp.float32)


def complex_product(first_side, second_side, pattern, precision):
    def part(i, j):
        return jnp.einsum(
            pattern,
            first_side[:, i],
            second_side[:, j],
            precision=precision,
            preferred_element_type=jnp.float32,
        )

    return jnp.stack([part(0, 0) - part(1, 1), part(0, 1) + part(1, 0)], axis=1)


def restrict(source, blocks, blocks_total):
    rows_within = source.shape[2] // blocks_total
    cols_within = source.shape[3] // blocks_total
    rows = one_hot_rows(blocks, blocks_total, rows_within)
    cols = one_hot_rows(blocks, blocks_total, cols_within)
    picked = jnp.einsum("bmk,bikn->bimn", rows, source, precision=EXACT)
    return jnp.einsum("bimn,bjn->bimj", picked, cols, precision=EXACT)


def my_columns(factor_columns, root_col):
    mine = lax.axis_index("col") == root_col
    return lax.psum(jnp.where(mine, factor_columns, jnp.zeros_like(factor_columns)), "col")


def supernodes(ancestors, mine, gathered, diagonal):
    coupled = -complex_product(mine, ancestors, "bkm,bkn->bmn", HIGH)
    coupled = lax.all_gather(coupled, "col", axis=3, tiled=True)
    return coupled, diagonal - complex_product(coupled, gathered, "bmk,bkn->bmn", HIGH)


def shards(
    top_inverse,
    blocks_upper,
    factor_upper,
    diagonal_upper,
    parents_lower,
    blocks_lower,
    factor_lower,
    diagonal_lower,
):
    row_devices = lax.axis_size("row")
    ratio = row_devices // lax.axis_size("col")
    rows_here = diagonal_upper.shape[2]
    my_row = lax.axis_index("row")
    root_col = my_row // ratio
    slice_start = my_row % ratio * rows_here
    across = factor_upper.shape[2] * row_devices
    kb = rows_here * row_devices // (across // blocks_upper.shape[1])
    ntb = top_inverse.shape[1] * row_devices // (across // blocks_upper.shape[1])

    source = jnp.broadcast_to(top_inverse, (blocks_upper.shape[0],) + top_inverse.shape)
    picked = restrict(source, blocks_upper, ntb)
    ancestors = lax.all_gather(picked, "row", axis=2, tiled=True)
    gathered_upper = lax.all_gather(factor_upper, "row", axis=2, tiled=True)
    gathered_lower = lax.all_gather(factor_lower, "row", axis=2, tiled=True)
    mine = my_columns(lax.dynamic_slice_in_dim(gathered_upper, slice_start, rows_here, 3), root_col)
    upper_coupling, upper_blocks = supernodes(ancestors, mine, gathered_upper, diagonal_upper)

    source = jnp.take(upper_blocks, parents_lower, axis=0)
    picked = restrict(source, blocks_lower, kb)
    ancestors = lax.all_gather(picked, "row", axis=2, tiled=True)
    mine = my_columns(lax.dynamic_slice_in_dim(gathered_lower, slice_start, rows_here, 3), root_col)
    lower_coupling, lower_blocks = supernodes(ancestors, mine, gathered_lower, diagonal_lower)
    return upper_coupling, upper_blocks, lower_coupling, lower_blocks


def solution(mesh):
    split = P(None, None, "row", "col")
    return jax.shard_map(
        shards,
        mesh=mesh,
        in_specs=(P(None, "row", "col"), P(), split, split, P(), P(), split, split),
        out_specs=(P(None, None, "row", None), split, P(None, None, "row", None), split),
        check_vma=False,
    )
```

time: 999 us -> 903 us (0.904)
  other arithmetic: 116 us -> 29.9 us
  local copies, waits for them, and re-layouts: 162 us -> 115 us
  matrix products: 91.1 us -> 125 us
    select_n x2 -> x1, other arithmetic: 64.7 us -> 0.01 us  [shards(): source = jnp.take(upper_blocks, parents_lower, axis=0)]
    gather x4 -> x3, local copies, waits for them, and re-layouts: 69.4 us -> 16.3 us  [shards(): source = jnp.take(upper_blocks, parents_lower, axis=0)]
    slice x0 -> x3, local copies, waits for them, and re-layouts: none -> 52.9 us  [the longest x2 52.8 us: part(): second_side[:, j]]
    gather x12 -> x0, local copies, waits for them, and re-layouts: 48.8 us -> none  [the longest x6 29.3 us: pick_single(): matrix = jnp.take(matrix, chosen, axis=4)]
    dot_general x4 -> x20, matrix products: 91.1 us -> 125 us  [the longest x16 102 us: part(): jnp.einsum(pattern, first_side[:, i], second_side[:, j], precision=precis...]
    broadcast_in_dim x7 -> x1, local copies, waits for them, and re-layouts: 17.4 us -> 0.01 us  [one_hot_rows(): jnp.where(rows % chosen_blocks == b, blocks[:, b, None, None], wanted)]
    unnamed x1 -> x2, other arithmetic: 11.6 us -> 0.01 us
    unnamed x20 -> x54, local copies, waits for them, and re-layouts: 25.9 us -> 37.1 us
  transfers between devices with their start and end apart: 7 -> 7, of which waited for: 7 -> 5; matrix products, arithmetic and copies ran while one was open for 5% -> 10% of each run, Pallas kernels for 0% -> 0%
where the time goes in v1:
time: 903 us; the launch traced here: 888 us
  waiting for transfers between devices  603 us (67%)
  matrix products  125 us (14%)
  local copies, waits for them, and re-layouts  115 us (13%)
  other arithmetic  29.9 us (3%)
  between operations  14.9 us (2%)
    all_gather x1, waiting for transfers between devices, shards(): gathered_lower = lax.all_gather(factor_lower, 'row', axis=2, tiled=True)  265 us
    all_gather x1, waiting for transfers between devices, shards(): gathered_upper = lax.all_gather(factor_upper, 'row', axis=2, tiled=True)  189 us
    all_gather x2, waiting for transfers between devices, shards(): ancestors = lax.all_gather(picked, 'row', axis=2, tiled=True)  117 us
    dot_general x16, matrix products, part(): jnp.einsum(pattern, first_side[:, i], second_side[:, j], precision=precis...  102 us
    slice x2, local copies, waits for them, and re-layouts, part(): second_side[:, j]  52.8 us
    unnamed x54, local copies, waits for them, and re-layouts  37.1 us
    psum x1, waiting for transfers between devices, my_columns(): lax.psum(jnp.where(mine, factor_columns, jnp.zeros_like(factor_columns)),...  32 us
    sub x2, other arithmetic, supernodes(): diagonal - complex_product(coupled, gathered, 'bmk,bkn->bmn', HIGH)  19.9 us
  transfers between devices with their start and end apart: 7, of which 5 were waited for; matrix products, arithmetic and copies ran while one was open for 10% of the time, Pallas kernels for 0%

profile of v1, /device:TPU:0, one launch (start us, length us, event | category | flops | bytes accessed | tf_op | source)
XLA Modules:
  0.0 888.3 jit_solution(12893786117642717030)
XLA Ops:
  16.5 189.2 %all-gather.7.cloned.1.call-done = f32[2,2,512,2048]{3,1,0,2:T(2,128)} async-done(((f32[2,2,32,2048]{3,1,0,2:T(2,128)}), f32[2,2,512,2048]{3,1,0,2:T(2,128)}) %all-gather.7.cloned.1.call-update) | async-done | bytes 16777232 | tf_op jit(solution)/shard_map/all_gather | solution.py:77
  213.8 264.7 %all-gather.13.cloned.1.call-done = f32[3,2,512,2048]{3,1,0,2:T(2,128)} async-done(((f32[3,2,32,2048]{3,1,0,2:T(2,128)}), f32[3,2,512,2048]{3,1,0,2:T(2,128)}) %all-gather.13.cloned.1.call-update) | async-done | bytes 25165840 | tf_op jit(solution)/shard_map/all_gather | solution.py:78
  478.5 4.6 constant_dynamic-slice_fusion
  493.2 47.7 %all-gather.9.cloned.1.call-done = f32[2,2,512,256]{3,2,1,0:T(8,128)} async-done(((f32[2,2,32,256]{3,2,1,0:T(8,128)}), f32[2,2,512,256]{3,2,1,0:T(8,128)}) %all-gather.9.cloned.1.call-update) | async-done | bytes 2097168 | tf_op jit(solution)/shard_map/all_gather | solution.py:76
  540.9 32.0 %all-reduce.3.cloned.1.call-done = (f32[2,2,512,256]{2,3,0,1:T(8,128)}, f32[3,2,512,256]{2,3,0,1:T(8,128)}) async-done(((f32[2,2,512,256]{2,3,0,1:T(8,128)}, f32[3,2,512,256]{2,3,0,1:T(8,128)}), (f32[2,2,512,256]{2,3,0,1:T(8,128)}, f32[3,2,512,256]{2,3,0,1:T(8,128)})) %all-reduce.3.cloned.1.call-update) | async-done | bytes 5242896 | tf_op jit(solution)/shard_map/psum | solution.py:45
  579.9 22.5 %fusion.115 = (f32[2,1,512,2048]{3,1,0,2:T(1,128)}, f32[2,1,512,2048]{3,1,0,2:T(1,128)}) fusion(f32[2,2,512,2048]{3,1,0,2:T(2,128)} %all-gather.7.cloned.1.call-done), kind=kLoop, calls=%fused_computation.203 | loop fusion | bytes 33554432 | tf_op jit(solution)/shard_map/slice | solution.py:26
  602.4 10.2 %fusion.8 = f32[2,256,2048]{2,1,0:T(8,128)S(1)} fusion(f32[2,1,512,2048]{3,1,0,2:T(1,128)} %get-tuple-element.19, f32[2,2,256,512]{3,2,0,1:T(8,128)} %all-gather.11.cloned.1.call-done), kind=kOutput, calls=%fused_computation.17 | convolution fusion | flops 3221225472 | bytes 13631488 | tf_op jit(solution)/shard_map/bmk,bkn->bmn/dot_general | solution.py:23
  612.7 9.8 %fusion.7 = f32[2,256,2048]{2,1,0:T(8,128)S(1)} fusion(f32[2,1,512,2048]{3,1,0,2:T(1,128)S(1)} %copy-done.3, f32[2,2,256,512]{3,2,0,1:T(8,128)} %all-gather.11.cloned.1.call-done), kind=kOutput, calls=%fused_computation.16 | convolution fusion | flops 3221225472 | bytes 13631488 | tf_op jit(solution)/shard_map/bmk,bkn->bmn/dot_general | solution.py:23
  622.5 9.0 %subtract_bitcast_fusion.1 = f32[2,1,256,2048]{3,2,0,1:T(8,128)} fusion(f32[2,256,2048]{2,1,0:T(8,128)S(1)} %fusion.8, f32[2,1,512,2048]{3,1,0,2:T(1,128)S(1)} %bitcast.137, f32[2,2,256,512]{3,2,0,1:T(8,128)S(1)} %copy-done.6), kind=kOutput, calls=%fused_computation.30 | convolution fusion | flops 3222274048 | bytes 17825792 | tf_op jit(solution)/shard_map/bmk,bkn->bmn/dot_general | solution.py:23
  631.5 9.2 %add_bitcast_fusion.1 = f32[2,1,256,2048]{3,2,0,1:T(8,128)} fusion(f32[2,256,2048]{2,1,0:T(8,128)S(1)} %fusion.7, f32[2,1,512,2048]{3,1,0,2:T(1,128)S(1)} %bitcast.137, f32[2,2,256,512]{3,2,0,1:T(8,128)S(1)} %copy-done.6), kind=kOutput, calls=%fused_computation.29 | convolution fusion | flops 3222274048 | bytes 17825792 | tf_op jit(solution)/shard_map/bmk,bkn->bmn/dot_general | solution.py:23
  640.7 5.5 maximum_subtract_fusion.1
  651.9 5.8 gather_fusion
  657.8 5.8 gather_fusion.1
  663.6 11.7 %fusion.27 = f32[3,2,32,2048]{3,2,1,0:T(8,128)S(1)} fusion(f32[3,2,256,1024]{3,2,1,0:T(8,128)} %gather_fusion.1, f32[3,2,256,1024]{3,2,1,0:T(8,128)} %gather_fusion, pred[3]{0:T(512)(128)(4,1)S(1)} %compare_and_fusion.1, s32[3]{0:T(128)S(1)} %get-tuple-element.31, s32[3]{0:T(128)S(1)} %get-tuple-element.30, s32[32,256]{1,0:T(8,128)S(1)} %broadcast_select_fusion.4, ...), kind=kOutput, calls=%fused_computation.42 | convolution fusion | flops 1214373888 | bytes 14213147 | tf_op jit(solution)/shard_map/bmk,bikn->bimn/dot_general | solution.py:39
  675.3 9.0 %fusion.11 = f32[3,2,32,256]{3,2,1,0:T(8,128)} fusion(f32[3,2,32,2048]{3,2,1,0:T(8,128)S(1)} %fusion.27, s32[3]{0:T(128)S(1)} %get-tuple-element.31, s32[3]{0:T(128)S(1)} %get-tuple-element.30, s32[256,2048]{1,0:T(8,128)S(1)} %copy-done.12, pred[256,2048]{1,0:T(8,128)(4,1)S(1)} %copy-done.14, pred[256,2048]{1,0:T(8,128)(4,1)S(1)} %get-tuple-element.22, ...), kind=kOutput, calls=%fused_computation.20 | convolution fusion | flops 1215823872 | bytes 5439512 | tf_op jit(solution)/shard_map/bimn,bjn->bimj/dot_general | solution.py:40
  684.4 69.7 %all-gather.15.cloned.1.call-done = f32[3,2,512,256]{3,2,1,0:T(8,128)} async-done(((f32[3,2,32,256]{3,2,1,0:T(8,128)}), f32[3,2,512,256]{3,2,1,0:T(8,128)}) %all-gather.15.cloned.1.call-update) | async-done | bytes 3145744 | tf_op jit(solution)/shard_map/all_gather | solution.py:84
  762.6 30.2 %fusion.114 = (f32[3,1,512,2048]{3,1,0,2:T(1,128)}, f32[3,1,512,2048]{3,1,0,2:T(1,128)}) fusion(f32[3,2,512,2048]{3,1,0,2:T(2,128)} %all-gather.13.cloned.1.call-done), kind=kLoop, calls=%fused_computation.202 | loop fusion | bytes 50331648 | tf_op jit(solution)/shard_map/slice | solution.py:26
  792.8 7.9 copy.39
  802.2 14.3 %fusion.4 = f32[3,256,2048]{2,1,0:T(8,128)} fusion(f32[3,1,512,2048]{3,1,0,2:T(1,128)} %get-tuple-element.17, f32[3,2,256,512]{3,2,0,1:T(8,128)} %all-gather.17.cloned.1.call-done), kind=kOutput, calls=%fused_computation.10 | convolution fusion | flops 4831838208 | bytes 20447232 | tf_op jit(solution)/shard_map/bmk,bkn->bmn/dot_general | solution.py:23
  816.5 12.4 %fusion.3 = f32[3,256,2048]{2,1,0:T(8,128)S(1)} fusion(f32[3,1,512,2048]{3,1,0,2:T(1,128)} %get-tuple-element.17, f32[3,2,256,512]{3,2,0,1:T(8,128)S(1)} %copy-done.4), kind=kOutput, calls=%fused_computation.9 | convolution fusion | flops 4831838208 | bytes 20447232 | tf_op jit(solution)/shard_map/bmk,bkn->bmn/dot_general | solution.py:23
  829.0 12.5 %subtract_bitcast_fusion = f32[3,1,256,2048]{3,2,0,1:T(8,128)} fusion(f32[3,256,2048]{2,1,0:T(8,128)} %fusion.4, f32[3,1,512,2048]{3,1,0,2:T(1,128)S(1)} %bitcast.135, f32[3,2,256,512]{3,2,0,1:T(8,128)} %all-gather.17.cloned.1.call-done), kind=kOutput, calls=%fused_computation.23 | convolution fusion | flops 4833411072 | bytes 26738688 | tf_op jit(solution)/shard_map/bmk,bkn->bmn/dot_general | solution.py:23
  841.5 11.7 %add_bitcast_fusion = f32[3,1,256,2048]{3,2,0,1:T(8,128)} fusion(f32[3,256,2048]{2,1,0:T(8,128)S(1)} %fusion.3, f32[3,1,512,2048]{3,1,0,2:T(1,128)S(1)} %bitcast.135, f32[3,2,256,512]{3,2,0,1:T(8,128)} %all-gather.17.cloned.1.call-done), kind=kOutput, calls=%fused_computation.22 | convolution fusion | flops 4833411072 | bytes 26738688 | tf_op jit(solution)/shard_map/bmk,bkn->bmn/dot_general | solution.py:23
  853.1 14.5 %maximum_subtract_fusion = f32[3,2,256,2048]{3,2,0,1:T(8,128)} fusion(f32[3,1,256,2048]{3,2,0,1:T(8,128)} %add_bitcast_fusion, f32[3,1,256,2048]{3,2,0,1:T(8,128)} %subtract_bitcast_fusion, f32[3,2,256,2048]{3,2,1,0:T(8,128)} %param.15), kind=kLoop, calls=%fused_computation.6 | loop fusion | flops 6291456 | bytes 37748736 | tf_op jit(solution)/shard_map/sub | solution.py:51
  867.6 11.7 %copy.41 = f32[3,2,256,2048]{3,2,1,0:T(8,128)} copy(f32[3,2,256,2048]{3,2,0,1:T(8,128)} %maximum_subtract_fusion) | data formatting | bytes 25165824
  (125 shorter events, 51.8 us)
Async XLA Ops:
  7.2 6.7 copy-start
  7.2 198.5 %all-gather.7.cloned.1.call-start = ((), (), s32[]{:S(2)}) async-start(), calls=%async_computation | async-start | bytes 17825792 | tf_op jit(solution)/shard_map/all_gather | solution.py:77
  10.4 468.1 %all-gather.13.cloned.1.call-start = ((), (), s32[]{:S(2)}) async-start(), calls=%async_computation.3 | async-start | bytes 26738688 | tf_op jit(solution)/shard_map/all_gather | solution.py:78
  12.8 528.1 %all-gather.9.cloned.1.call-start = ((), (), s32[]{:S(2)}) async-start(), calls=%async_computation.1 | async-start | bytes 2228224 | tf_op jit(solution)/shard_map/all_gather | solution.py:76
  16.4 556.5 %all-reduce.3.cloned.1.call-start = ((), (), s32[]{:S(2)}) async-start(), calls=%async_computation.6 | async-start | bytes 10485760 | tf_op jit(solution)/shard_map/psum | solution.py:45
  489.2 113.2 %all-gather.11.cloned.1.call-start = ((), (), s32[]{:S(2)}) async-start(), calls=%async_computation.2 | async-start | bytes 3145728 | tf_op jit(solution)/shard_map/all_gather | solution.py:50
  540.9 34.3 %copy-start.10 = (f32[2,2,512,256]{3,2,1,0:T(8,128)S(1)}, f32[2,2,512,256]{3,2,1,0:T(8,128)}, u32[]{:S(2)}) copy-start(f32[2,2,512,256]{3,2,1,0:T(8,128)} %all-gather.9.cloned.1.call-done) | copy-start | bytes 6291460
  579.5 174.6 %all-gather.15.cloned.1.call-start = ((), (), s32[]{:S(2)}) async-start(), calls=%async_computation.4 | async-start | bytes 3342336 | tf_op jit(solution)/shard_map/all_gather | solution.py:84
  602.4 10.2 %copy-start.3 = (f32[2,1,512,2048]{3,1,0,2:T(1,128)S(1)}, f32[2,1,512,2048]{3,1,0,2:T(1,128)}, u32[]{:S(2)}) copy-start(f32[2,1,512,2048]{3,1,0,2:T(1,128)} %get-tuple-element.19) | copy-start | bytes 25165828
  602.4 20.0 %slice-start.3 = ((s8[8388608]{0:T(1024)(128)(4,1)}), s8[4194304]{0:T(1024)(128)(4,1)S(1)}, s32[]{:S(2)}) async-start(s8[8388608]{0:T(1024)(128)(4,1)} %bitcast.136), calls=%async_computation.10 | async-start | bytes 8388608
  612.6 9.8 %slice-start.4 = ((s8[8388608]{0:T(1024)(128)(4,1)}), s8[4194304]{0:T(1024)(128)(4,1)S(1)}, s32[]{:S(2)}) async-start(s8[8388608]{0:T(1024)(128)(4,1)} %bitcast.136), calls=%async_computation.11 | async-start | bytes 8388608
  612.7 9.8 %copy-start.6 = (f32[2,2,256,512]{3,2,0,1:T(8,128)S(1)}, f32[2,2,256,512]{3,2,0,1:T(8,128)}, u32[]{:S(2)}) copy-start(f32[2,2,256,512]{3,2,0,1:T(8,128)} %all-gather.11.cloned.1.call-done) | copy-start | bytes 6291460
  631.5 9.2 %copy-start.7 = (f32[2,1,256,2048]{3,2,0,1:T(8,128)S(1)}, f32[2,1,256,2048]{3,2,0,1:T(8,128)}, u32[]{:S(2)}) copy-start(f32[2,1,256,2048]{3,2,0,1:T(8,128)} %subtract_bitcast_fusion.1) | copy-start | bytes 12582916
  646.1 5.8 copy-start.2
  663.6 11.7 %copy-start.12 = (s32[256,2048]{1,0:T(8,128)S(1)}, s32[256,2048]{1,0:T(8,128)}, u32[]{:S(2)}) copy-start(s32[256,2048]{1,0:T(8,128)} %broadcast_select_fusion.1) | copy-start | bytes 6291460
  663.6 11.7 %copy-start.14 = (pred[256,2048]{1,0:T(8,128)(4,1)S(1)}, pred[256,2048]{1,0:T(8,128)(4,1)}, u32[]{:S(2)}) copy-start(pred[256,2048]{1,0:T(8,128)(4,1)} %get-tuple-element.23) | copy-start | bytes 1572868
  684.3 117.9 %all-gather.17.cloned.1.call-start = ((), (), s32[]{:S(2)}) async-start(), calls=%async_computation.5 | async-start | bytes 4718592 | tf_op jit(solution)/shard_map/all_gather | solution.py:50
  754.0 5.3 copy-start.9
  802.2 14.3 %copy-start.4 = (f32[3,2,256,512]{3,2,0,1:T(8,128)S(1)}, f32[3,2,256,512]{3,2,0,1:T(8,128)}, u32[]{:S(2)}) copy-start(f32[3,2,256,512]{3,2,0,1:T(8,128)} %all-gather.17.cloned.1.call-done) | copy-start | bytes 9437188
  802.2 26.7 %slice-start = ((s8[12582912]{0:T(1024)(128)(4,1)}), s8[4194304]{0:T(1024)(128)(4,1)S(1)}, s32[]{:S(2)}) async-start(s8[12582912]{0:T(1024)(128)(4,1)} %bitcast.134), calls=%async_computation.7 | async-start | bytes 8388608
  802.2 26.7 %slice-start.1 = ((s8[12582912]{0:T(1024)(128)(4,1)}), s8[4194304]{0:T(1024)(128)(4,1)S(1)}, s32[]{:S(2)}) async-start(s8[12582912]{0:T(1024)(128)(4,1)} %bitcast.134), calls=%async_computation.8 | async-start | bytes 8388608
  816.5 12.4 %slice-start.2 = ((s8[12582912]{0:T(1024)(128)(4,1)}), s8[4194304]{0:T(1024)(128)(4,1)S(1)}, s32[]{:S(2)}) async-start(s8[12582912]{0:T(1024)(128)(4,1)} %bitcast.134), calls=%async_computation.9 | async-start | bytes 8388608
  867.6 11.7 %copy-start.5 = (f32[3,2,256,512]{3,2,0,1:T(8,128)S(1)}, f32[3,2,256,512]{3,2,0,1:T(8,128)}, u32[]{:S(2)}) copy-start(f32[3,2,256,512]{3,2,0,1:T(8,128)} %all-gather.17.cloned.1.call-done) | copy-start | bytes 9437188
  867.6 13.7 %copy-start.1 = (f32[2,64,512]{2,1,0:T(8,128)S(1)}, f32[2,64,512]{2,1,0:T(8,128)}, u32[]{:S(2)}) copy-start(f32[2,64,512]{2,1,0:T(8,128)} %param.8) | copy-start | bytes 786436
  (6 other events, 14.4 us)
Sparse Core Ops, SparseCore 0:
  11.4 194.3 all-gather.6
  209.1 269.4 all-gather.12
  481.8 59.0 all-gather.8
  543.9 28.9 all-reduce.2
  579.6 11.7 all-gather.10
  684.4 69.5 all-gather.14
  762.7 10.9 all-gather.16

commit v2 on v0

--- a/solution.py
+++ b/solution.py
@@ -1,6 +1,8 @@
 import jax
 import jax.numpy as jnp
 from jax import lax
+from jax.experimental import pallas as pl
+from jax.experimental.pallas import tpu as pltpu
 from jax.sharding import PartitionSpec as P
 
 BS = 256
@@ -98,6 +100,341 @@
     return (upper_coupling, upper_blocks, coupling_out, block_out)
 
 
+NZ, NY, NX = 4, 2, 2
+TILE = 256
+ROUTES = (("zyx", 0, 640), ("zxy", 640, 640), ("xzy", 1280, 384), ("yzx", 1664, 384))
+SMALL = (("zyx", 0, 128), ("zxy", 128, 128))
+EXACT = lax.Precision.HIGHEST
+
+
+def split(value):
+    high = value.astype(jnp.bfloat16)
+    return high, (value - high.astype(jnp.float32)).astype(jnp.bfloat16)
+
+
+def dot(a, b):
+    return jnp.dot(a, b, preferred_element_type=jnp.float32)
+
+
+def dot3(a, b):
+    return dot(a[0], b[0]) + (dot(a[0], b[1]) + dot(a[1], b[0]))
+
+
+def fused(
+    fu, fl, au, du, dl, pick, ends,
+    ct_out, b_out, gathered,
+    anc, mine, ct, left, gbuf, dbuf, obuf, picked,
+    fsend, frecv, asend, arecv, msend, mrecv, mlocal, csend, crecv, own_sem, tile_in, tile_out, ct_sem,
+):
+    row, col = lax.axis_index("row"), lax.axis_index("col")
+    z, y, x = row // (NY * NX), row // NX % NY, row % NX
+    root = row // 8
+    place = {"z": z, "y": y, "x": x}
+    size = {"z": NZ, "y": NY, "x": NX}
+
+    def device(dim, step):
+        at = dict(place)
+        at[dim] = lax.rem(at[dim] + step, size[dim])
+        return (at["z"] * (NY * NX) + at["y"] * NX + at["x"], col)
+
+    other = (row, 1 - col)
+    barrier = pltpu.get_barrier_semaphore()
+    peers = [device("z", 1), device("z", 2), device("z", 3), device("y", 1), device("x", 1), other]
+    for peer in peers:
+        pl.semaphore_signal(barrier, inc=1, device_id=peer, device_id_type=pl.DeviceIdType.MESH)
+    pl.semaphore_wait(barrier, len(peers))
+
+    def region(buf, number, full, cols):
+        at = [slice(None) if d in full else pl.ds(place[d], 1) for d in "zyx"]
+        return buf.at[pl.ds(2 * number, 2), at[0], at[1], at[2], :, cols]
+
+    def messages(buf, routes, send, recv, number, phase):
+        made = []
+        for r, (order, first, width) in enumerate(routes):
+            dim = order[phase]
+            ref = region(buf, number, order[:phase], pl.ds(first, width))
+            for step in range(1, size[dim]):
+                sem = (number, r, {"z": 0, "y": 3, "x": 4}[dim] + step - 1)
+                made.append(
+                    pltpu.make_async_remote_copy(
+                        src_ref=ref,
+                        dst_ref=ref,
+                        send_sem=send.at[sem],
+                        recv_sem=recv.at[sem],
+                        device_id=device(dim, step),
+                        device_id_type=pl.DeviceIdType.MESH,
+                    )
+                )
+        return made
+
+    pending = []
+
+    def start(made):
+        for m in made:
+            m.start()
+        pending.extend(made)
+
+    def arrive(made):
+        for m in made:
+            m.wait_recv()
+
+    def f_msg(number, phase):
+        return messages(gathered, ROUTES, fsend, frecv, number, phase)
+
+    def a_msg(numbers, phase):
+        made = []
+        for number in numbers:
+            made += messages(anc, SMALL, asend, arecv, number, phase)
+        return made
+
+    upper, lower = fu.shape[0] // 2, fl.shape[0] // 2
+    total = upper + lower
+    ups, lows = range(upper), range(upper, total)
+    whole = pl.ds(0, fu.shape[5])
+
+    locals_ = []
+    for s in range(total):
+        src = fu.at[pl.ds(2 * s, 2)] if s < upper else fl.at[pl.ds(2 * (s - upper), 2)]
+        locals_.append(pltpu.make_async_copy(src, region(gathered, s, "", whole), own_sem.at[s]))
+    for s in ups:
+        locals_.append(pltpu.make_async_copy(au.at[pl.ds(2 * s, 2)], region(anc, s, "", pl.ds(0, 256)), own_sem.at[total + s]))
+    for c in locals_:
+        c.start()
+    for c in locals_:
+        c.wait()
+
+    def move_mine(s):
+        columns = pl.ds(pl.multiple_of(lax.rem(row, 8) * TILE, TILE), TILE)
+        src = gathered.at[pl.ds(2 * s, 2), :, :, :, :, columns]
+        remote = pltpu.make_async_remote_copy(
+            src_ref=src, dst_ref=mine.at[s], send_sem=msend.at[s], recv_sem=mrecv.at[s],
+            device_id=other, device_id_type=pl.DeviceIdType.MESH,
+        )
+
+        @pl.when(col == root)
+        def _():
+            remote.start()
+            here = pltpu.make_async_copy(src, mine.at[s], mlocal.at[s])
+            here.start()
+            here.wait()
+            remote.wait_send()
+
+        @pl.when(col != root)
+        def _():
+            remote.wait_recv()
+
+    def compute(s):
+        is_upper = s < upper
+        diag = du if is_upper else dl
+        d_at = s if is_upper else s - upper
+        move_mine(s)
+        turned = split(mine[s].reshape(1024, TILE).T)
+        a_all = anc[2 * s : 2 * s + 2].reshape(2, 512, TILE)
+        ar, ai = a_all[0], a_all[1]
+        right = jnp.concatenate(
+            [jnp.concatenate([-ar, -ai], axis=1), jnp.concatenate([ai, -ar], axis=1)], axis=0
+        )
+        half = dot3(turned, split(right))
+        cols = pl.ds(pl.multiple_of(col * TILE, TILE), TILE)
+        ct[s, 0, :, cols] = half[:, :TILE]
+        ct[s, 1, :, cols] = half[:, TILE:]
+        swap = pltpu.make_async_remote_copy(
+            src_ref=ct.at[s, :, :, cols], dst_ref=ct.at[s, :, :, cols],
+            send_sem=csend.at[s], recv_sem=crecv.at[s],
+            device_id=other, device_id_type=pl.DeviceIdType.MESH,
+        )
+        swap.start()
+        swap.wait()
+        out = pltpu.make_async_copy(ct.at[s], ct_out.at[s], ct_sem)
+        out.start()
+        cr, ci = split(ct[s, 0]), split(ct[s, 1])
+        for k in range(2):
+            left[k, :TILE, :512] = cr[k]
+            left[k, :TILE, 512:] = -ci[k]
+            left[k, TILE:, :512] = ci[k]
+            left[k, TILE:, 512:] = cr[k]
+
+        tiles = fu.shape[5] // TILE
+
+        def span(n):
+            return pl.ds(n * TILE if isinstance(n, int) else pl.multiple_of(n * TILE, TILE), TILE)
+
+        def loads(n, slot):
+            return (
+                pltpu.make_async_copy(gathered.at[pl.ds(2 * s, 2), :, :, :, :, span(n)], gbuf.at[slot], tile_in.at[0, slot]),
+                pltpu.make_async_copy(diag.at[d_at, :, :, span(n)], dbuf.at[slot], tile_in.at[1, slot]),
+            )
+
+        def store(n, slot):
+            return pltpu.make_async_copy(obuf.at[slot], b_out.at[s, :, :, span(n)], tile_out.at[slot])
+
+        for c in loads(0, 0):
+            c.start()
+
+        @pl.loop(0, tiles)
+        def _(n):
+            slot = lax.rem(n, 2)
+
+            @pl.when(n + 1 < tiles)
+            def _():
+                for c in loads(n + 1, 1 - slot):
+                    c.start()
+
+            for c in loads(n, slot):
+                c.wait()
+
+            @pl.when(n >= 2)
+            def _():
+                store(n - 2, slot).wait()
+
+            rows = split(gbuf[slot].reshape(1024, TILE))
+            block = dbuf[slot].reshape(512, TILE) - dot3((left[0], left[1]), rows)
+            obuf[slot] = block.reshape(2, TILE, TILE)
+            store(n, slot).start()
+            if is_upper:
+                for k in range(2):
+                    parts = split(block[k * TILE : (k + 1) * TILE])
+                    chosen = dot(pick[s], parts[0]) + dot(pick[s], parts[1])
+                    if s == 0:
+                        picked[k, :, span(n)] = chosen
+                    else:
+                        picked[k, :, span(n)] += chosen
+
+        store(tiles - 2, 0).wait()
+        store(tiles - 1, 1).wait()
+        out.wait()
+
+    def pick_lower():
+        for t in range(lower):
+            for k in range(2):
+                for h in range(2):
+                    rows = split(picked[k, 32 * t : 32 * t + 32, 1024 * h : 1024 * h + 1024])
+                    value = dot(rows[0], ends[t]) + dot(rows[1], ends[t])
+                    anc[2 * (upper + t) + k, z, y, x, :, 128 * h : 128 * h + 128] = value
+
+    start(a_msg(ups, 0))
+    start(f_msg(0, 0))
+    start(f_msg(1, 0))
+    arrive(a_msg(ups, 0))
+    start(a_msg(ups, 1))
+    arrive(f_msg(0, 0))
+    start(f_msg(0, 1))
+    start(f_msg(2, 0))
+    arrive(a_msg(ups, 1))
+    start(a_msg(ups, 2))
+    arrive(f_msg(1, 0))
+    start(f_msg(1, 1))
+    arrive(f_msg(0, 1))
+    start(f_msg(0, 2))
+    start(f_msg(3, 0))
+    arrive(f_msg(2, 0))
+    start(f_msg(2, 1))
+    arrive(f_msg(1, 1))
+    start(f_msg(1, 2))
+    start(f_msg(4, 0))
+    arrive(a_msg(ups, 2))
+    arrive(f_msg(0, 2))
+    compute(0)
+    arrive(f_msg(3, 0))
+    start(f_msg(3, 1))
+    arrive(f_msg(1, 2))
+    compute(1)
+    pick_lower()
+    start(a_msg(lows, 0))
+    arrive(f_msg(2, 1))
+    start(f_msg(2, 2))
+    arrive(f_msg(4, 0))
+    start(f_msg(4, 1))
+    arrive(a_msg(lows, 0))
+    start(a_msg(lows, 1))
+    arrive(f_msg(3, 1))
+    start(f_msg(3, 2))
+    arrive(a_msg(lows, 1))
+    start(a_msg(lows, 2))
+    arrive(f_msg(4, 1))
+    start(f_msg(4, 2))
+    arrive(a_msg(lows, 2))
+    arrive(f_msg(2, 2))
+    compute(2)
+    arrive(f_msg(3, 2))
+    compute(3)
+    arrive(f_msg(4, 2))
+    compute(4)
+    for m in pending:
+        m.wait_send()
+
+
+def one_hot_rows(blocks, blocks_total, inner):
+    chosen_blocks = blocks.shape[1]
+    shape = (inner * chosen_blocks, inner * blocks_total)
+    rows = lax.broadcasted_iota(jnp.int32, shape, 0)
+    cols = lax.broadcasted_iota(jnp.int32, shape, 1)
+    wanted = jnp.zeros((blocks.shape[0],) + shape, jnp.int32)
+    for b in range(chosen_blocks):
+        wanted = jnp.where(rows % chosen_blocks == b, blocks[:, b, None, None], wanted)
+    same = rows // chosen_blocks == cols // blocks_total
+    return jnp.where(same & (cols % blocks_total == wanted), 1.0, 0.0).astype(jnp.float32)
+
+
+def fused_shards(top_inverse, blocks_upper, factor_upper, diagonal_upper, parents_lower, blocks_lower, factor_lower, diagonal_lower):
+    upper, lower = factor_upper.shape[0], factor_lower.shape[0]
+    total = upper + lower
+    width = factor_upper.shape[3]
+    rows = one_hot_rows(blocks_upper, NTB, top_inverse.shape[1] // NTB)
+    cols = one_hot_rows(blocks_upper, NTB, top_inverse.shape[2] // NTB)
+    au = jnp.einsum("bmk,ikn->bimn", rows, top_inverse, precision=EXACT)
+    au = jnp.einsum("bimn,bjn->bimj", au, cols, precision=EXACT)
+    rows = one_hot_rows(blocks_lower, KB, 16)
+    mine = (parents_lower[None, :] == jnp.arange(upper)[:, None]).astype(jnp.float32)
+    pick = (mine[:, :, None, None] * rows[None]).reshape(upper, lower * 32, 256).astype(jnp.bfloat16)
+    ends = jnp.swapaxes(one_hot_rows(blocks_lower, KB, 64), 1, 2).astype(jnp.bfloat16)
+
+    def cut(value):
+        return value.reshape(-1, 1, 1, 1, 32, value.shape[-1])
+
+    spec = pl.BlockSpec(memory_space=pl.ANY)
+    inside = pl.BlockSpec(memory_space=pltpu.VMEM)
+    f32, bf16 = jnp.float32, jnp.bfloat16
+    dma = pltpu.SemaphoreType.DMA
+    ct, block, _ = pl.pallas_call(
+        fused,
+        out_shape=(
+            jax.ShapeDtypeStruct((total, 2, 256, 512), f32),
+            jax.ShapeDtypeStruct((total, 2, 256, width), f32),
+            jax.ShapeDtypeStruct((2 * total, NZ, NY, NX, 32, width), f32),
+        ),
+        in_specs=[spec] * 5 + [inside] * 2,
+        out_specs=(spec,) * 3,
+        scratch_shapes=[
+            pltpu.VMEM((2 * total, NZ, NY, NX, 32, TILE), f32),
+            pltpu.VMEM((total, 2, NZ, NY, NX, 32, TILE), f32),
+            pltpu.VMEM((total, 2, 256, 512), f32),
+            pltpu.VMEM((2, 512, 1024), bf16),
+            pltpu.VMEM((2, 2, NZ, NY, NX, 32, TILE), f32),
+            pltpu.VMEM((2, 2, TILE, TILE), f32),
+            pltpu.VMEM((2, 2, TILE, TILE), f32),
+            pltpu.VMEM((2, lower * 32, width), f32),
+            dma((total, 4, 5)),
+            dma((total, 4, 5)),
+            dma((total, 2, 5)),
+            dma((total, 2, 5)),
+            dma((total,)),
+            dma((total,)),
+            dma((total,)),
+            dma((total,)),
+            dma((total,)),
+            dma((total + upper,)),
+            dma((2, 2)),
+            dma((2,)),
+            dma,
+        ],
+        compiler_params=pltpu.CompilerParams(
+            collective_id=0, has_side_effects=True, vmem_limit_bytes=52 * 1024 * 1024
+        ),
+    )(cut(factor_upper), cut(factor_lower), cut(au), diagonal_upper, diagonal_lower, pick, ends)
+    return ct[:upper], block[:upper], ct[upper:], block[upper:]
+
+
 def solution(mesh):
     placed = (
         P(None, "row", "col"),
@@ -109,8 +446,9 @@
         P(None, None, "row", "col"),
         P(None, None, "row", "col"),
     )
+    fits = dict(mesh.shape) == {"row": NZ * NY * NX, "col": 2}
     return jax.shard_map(
-        shards,
+        fused_shards if fits else shards,
         mesh=mesh,
         in_specs=placed,
         out_specs=(

time: 999 us -> 583 us (0.58)
  waiting for transfers between devices: 607 us -> 0 us
  Pallas kernels: 0 us -> 544 us
  local copies, waits for them, and re-layouts: 162 us -> 28.9 us
  other arithmetic: 116 us -> 3.71 us
  matrix products: 91.1 us -> 1.86 us
  between operations: 14.8 us -> 0.92 us
    all_gather x6 -> x0, waiting for transfers between devices: 574 us -> none  [the longest x2 435 us: supernode_level(): gathered_factor = lax.all_gather(factor_rows, 'row', axis=2, tiled=True)]
    pallas_call x0 -> x1, Pallas kernels: none -> 544 us  [fused_shards(): pl.pallas_call(fused, out_shape=(jax.ShapeDtypeStruct((total, 2, 256, 512...]
    gather x16 -> x0, local copies, waits for them, and re-layouts: 118 us -> none  [the longest x4 69.4 us: shards(): source = jnp.take(upper_blocks, parents_lower, axis=0)]
    dot_general x4 -> x2, matrix products: 91.1 us -> 1.86 us  [the longest x1 1.43 us: fused_shards(): au = jnp.einsum('bimn,bjn->bimj', au, cols, precision=EXACT)]
    select_n x8 -> x5, other arithmetic: 73.5 us -> 0.64 us  [the longest x4 0.53 us: one_hot_rows(): cols % blocks_total == wanted]
    psum x1 -> x0, waiting for transfers between devices: 32 us -> none  [from_root(): return lax.psum(block, axis)]
    slice x0 -> x5, local copies, waits for them, and re-layouts: none -> 27.6 us  [the longest x4 26.7 us: fused_shards(): return (ct[:upper], block[:upper], ct[upper:], block[upper:])]
    unnamed x20 -> x4, local copies, waits for them, and re-layouts: 25.9 us -> 0.02 us
  transfers between devices with their start and end apart: 7 -> 0, of which waited for: 7 -> 0; matrix products, arithmetic and copies ran while one was open for 5% -> 0% of each run, Pallas kernels for 0% -> 0%
where the time goes in v2:
time: 583 us; the launch traced here: 579 us
  Pallas kernels  544 us (93%)
  local copies, waits for them, and re-layouts  28.9 us (5%)
    pallas_call x1, Pallas kernels, fused_shards(): pl.pallas_call(fused, out_shape=(jax.ShapeDtypeStruct((total, 2, 256, 512...  544 us
    slice x4, local copies, waits for them, and re-layouts, fused_shards(): return (ct[:upper], block[:upper], ct[upper:], block[upper:])  26.7 us

profile of v2, /device:TPU:0, one launch (start us, length us, event | category | flops | bytes accessed | tf_op | source)
XLA Modules:
  0.0 579.4 jit_solution(6441458837773393211)
XLA Ops:
  0.8 0.7 compare_convert_fusion
  1.5 1.0 slice_reduce_fusion.1
  2.4 0.8 slice_bitcast_fusion.1
  3.3 0.1 broadcast_in_dim.176
  3.5 0.1 broadcast_in_dim.182
  3.6 0.1 select_compare_fusion.14
  3.7 0.1 mul.19
  3.8 0.1 select_compare_fusion.10
  3.9 0.1 select_compare_fusion.13
  4.1 0.1 select_compare_fusion.9
  4.2 0.1 fusion.17
  4.3 0.1 multiply_convert_fusion.pick
  4.4 0.9 select_compare_fusion.6
  5.3 0.2 select_compare_fusion.7
  5.5 0.4 convolution_bitcast_fusion
  5.9 0.2 select_compare_fusion.5
  6.2 0.5 broadcast_select_fusion
  6.6 0.6 select_convert_fusion.ends
  7.3 1.4 fusion.1
  8.7 544.0 %shard_map.111 = (f32[5,2,256,512]{3,2,1,0:T(8,128)}, f32[5,2,256,2048]{3,2,1,0:T(8,128)}, f32[10,4,2,2,32,2048]{5,4,3,2,1,0:T(8,128)}) custom-call(f32[4,1,1,1,32,2048]{5,4,3,2,1,0:T(8,128)} %bitcast.37, f32[6,1,1,1,32,2048]{5,4,3,2,1,0:T(8,128)} %bitcast.36, f32[4,1,1,1,32,256]{5,4,3,2,1,0:T(8,128)S(1)} %bitcast.35, f32[2,2,256,2048]{3,2,1,0:T(8,128)} %du.1, ...), custom_call_target="tpu_custom_call" | custom-call | tf_op jit(solution)/shard_map/pallas_call | solution.py:399
  552.7 3.1 slice.32
  555.8 4.1 slice.34
  559.9 7.9 %slice.33 = f32[2,2,256,2048]{3,2,1,0:T(8,128)} slice(f32[5,2,256,2048]{3,2,1,0:T(8,128)} %get-tuple-element.7), slice={[0:2], [0:2], [0:256], [0:2048]} | slice | bytes 16777216 | tf_op jit(solution)/shard_map/slice | solution.py:435
  567.8 11.6 %slice.35 = f32[3,2,256,2048]{3,2,1,0:T(8,128)} slice(f32[5,2,256,2048]{3,2,1,0:T(8,128)} %get-tuple-element.7), slice={[2:5], [0:2], [0:256], [0:2048]} | slice | bytes 25165824 | tf_op jit(solution)/shard_map/slice | solution.py:435
  (39 shorter events, 0.5 us)
Async XLA Ops:
  0.6 4.8 copy-start
  567.8 11.6 %copy-start.1 = (f32[2,64,512]{2,1,0:T(8,128)S(1)}, f32[2,64,512]{2,1,0:T(8,128)}, u32[]{:S(2)}) copy-start(f32[2,64,512]{2,1,0:T(8,128)} %param.8) | copy-start | bytes 786436
